TPU v7x, 128 devices: a whole 4x4x4 slice. The times are simulated.
128 devices in a mesh: pipe: 8 (over y, z_lo), rep: 16 (over z_hi, x, core).
Axes of the slice: x: 4, y: 4, z: 4 (z_hi: 2, z_lo: 2; z = z_hi * 2 + z_lo), core: 2. Of those that a mesh axis runs over, the one named last changes fastest.
Arguments:
- activations: bfloat16 [8, 2, 2048, 14336], P('pipe', None, 'rep'), may hold values from -6 to 6
- upstream: bfloat16 [8, 2048, 14336], P('pipe', 'rep'), may hold values from -6 to 6
- final_grad: bfloat16 [2048, 14336], P('rep'), may hold values from -6 to 6
- w_in: bfloat16 [8, 64, 14336], P('pipe'), may hold values from -0.375 to 0.375
- w_out: bfloat16 [8, 64, 14336], P('pipe'), may hold values from -0.375 to 0.375
- momentum: bfloat16 [8, 2, 64, 14336], P('pipe'), may hold values from -80 to 80
- worker_error: bfloat16 [8, 16, 2, 64, 14336], P('pipe', 'rep'), may hold values from -8 to 8
- server_error: bfloat16 [8, 2, 64, 14336], P('pipe', None, None, 'rep'), may hold values from -8 to 8
Outputs:
- input_grads: bfloat16 [8, 2048, 14336], P('pipe', 'rep')
- new_momentum: bfloat16 [8, 2, 64, 14336], P('pipe')
- new_worker_error: bfloat16 [8, 16, 2, 64, 14336], P('pipe', 'rep')
- new_server_error: bfloat16 [8, 2, 64, 14336], P('pipe', None, None, 'rep')
All inputs are finite; a program needn't handle non-finite values.
Results may differ from a plain program's by a relative error of at most 0.029.
Values may be sent and summed in bfloat16 or wider, within the bound.
A program may use at most 192 MiB of HBM per device.

v0:
```python
import jax
import jax.numpy as jnp
from jax import lax
from jax.sharding import PartitionSpec as P

GRP = 128


MOMENTUM_DECAY = 0.9
EPSILON = 1e-06
GELU_ROOT = 0.7978845608028654


def passed_along(value, axis, steps):
    count = lax.axis_size(axis)
    initial, last = (max(0, -steps), min(count, count - steps))
    return lax.ppermute(value, axis, [(source, source + steps) for source in range(initial, last)])


def gelu_parts(hidden):
    argument = GELU_ROOT * (hidden + 0.044715 * hidden * hidden * hidden)
    tangent = jnp.tanh(argument)
    gelu_value = 0.5 * hidden * (1.0 + tangent)
    gelu_slope = 0.5 * (1.0 + tangent) + 0.5 * hidden * (1.0 - tangent * tangent) * GELU_ROOT * (
        1.0 + 3.0 * 0.044715 * hidden * hidden
    )
    return (gelu_value, gelu_slope)


def compress(values):
    layout = values.shape
    grouped = values.reshape(layout[:-1] + (layout[-1] // GRP, GRP))
    scales = (jnp.mean(jnp.abs(grouped), axis=-1) + EPSILON).astype(jnp.bfloat16)
    widened = scales.astype(jnp.float32)[..., None]
    levels = jnp.clip(grouped / widened, -1.0, 1.0).astype(jnp.bfloat16)
    leftover = grouped - widened * levels.astype(jnp.float32)
    return (scales, levels.reshape(layout), leftover.reshape(layout))


def forward_slice(features, weight_in, weight_out, incoming):
    hidden = jnp.einsum("td,kd->tk", features, weight_in, preferred_element_type=jnp.float32)
    gelu_value, gelu_slope = gelu_parts(hidden)
    upward = jnp.einsum("td,kd->tk", incoming, weight_out, preferred_element_type=jnp.float32)
    return (gelu_value.astype(jnp.bfloat16), (upward * gelu_slope).astype(jnp.bfloat16))


def outer_sum(left, right):
    return jnp.einsum("tk,td->kd", left, right, preferred_element_type=jnp.float32)


def to_blocks(levels, scales, replicas):
    matrices, hidden_units, columns = levels.shape
    return (
        levels.reshape(matrices, hidden_units, replicas, columns // replicas),
        scales.reshape(matrices, hidden_units, replicas, scales.shape[2] // replicas),
    )


def serve_blocks(received_levels, received_scales, server_part):
    matrices, hidden_units, replicas, columns = received_levels.shape
    groups = columns // GRP
    weighted = received_scales.astype(jnp.float32)[..., None] * received_levels.astype(
        jnp.float32
    ).reshape(matrices, hidden_units, replicas, groups, GRP)
    average = (jnp.sum(weighted, axis=2) / replicas).reshape(matrices, hidden_units, columns)
    combined = average + server_part.astype(jnp.float32)
    server_scales, server_levels, server_left = compress(combined)
    return (server_levels, server_scales, server_left.astype(jnp.bfloat16))


def restore(levels, scales):
    matrices, hidden_units, columns = levels.shape
    groups = columns // GRP
    widened = scales.astype(jnp.float32)[..., None] * levels.astype(jnp.float32).reshape(
        matrices, hidden_units, groups, GRP
    )
    return widened.reshape(matrices, hidden_units, columns).astype(jnp.bfloat16)


def body(activations, upstream, final_grad, w_in, w_out, momentum, worker_error, server_error):
    first_rows = activations[0, 0]
    second_rows = activations[0, 1]
    weight_in = w_in[0]
    weight_out = w_out[0]
    first_incoming = upstream[0]
    first_gelu, first_grad = forward_slice(first_rows, weight_in, weight_out, first_incoming)
    passed = jnp.dot(first_grad, weight_in, preferred_element_type=jnp.float32).astype(jnp.bfloat16)
    arrived = passed_along(passed, "pipe", -1)
    is_last = lax.axis_index("pipe") == lax.axis_size("pipe") - 1
    second_incoming = jnp.where(is_last, final_grad, arrived)
    second_gelu, second_grad = forward_slice(second_rows, weight_in, weight_out, second_incoming)
    previous = momentum[0].astype(jnp.float32)
    carried = worker_error[0, 0].astype(jnp.float32)
    server_part = server_error[0]
    grad_out = outer_sum(first_gelu, first_incoming) + outer_sum(second_gelu, second_incoming)
    input_grads = jnp.dot(second_grad, weight_in, preferred_element_type=jnp.float32).astype(
        jnp.bfloat16
    )
    grad_in = outer_sum(first_grad, first_rows) + outer_sum(second_grad, second_rows)
    replicas = lax.axis_size("rep")
    gradient = jnp.stack([grad_in, grad_out], axis=0)
    blended = MOMENTUM_DECAY * previous + (1.0 - MOMENTUM_DECAY) * gradient + carried
    scales, levels, leftover = compress(blended)
    block_levels, block_scales = to_blocks(levels, scales, replicas)
    received_levels, received_scales = (
        lax.all_to_all(block_levels, "rep", split_axis=2, concat_axis=2, tiled=True),
        lax.all_to_all(block_scales, "rep", split_axis=2, concat_axis=2, tiled=True),
    )
    server_levels, server_scales, new_server = serve_blocks(
        received_levels, received_scales, server_part
    )
    full_levels, full_scales = (
        lax.all_gather(server_levels, "rep", axis=2, tiled=True),
        lax.all_gather(server_scales, "rep", axis=2, tiled=True),
    )
    new_momentum = restore(full_levels, full_scales)
    new_worker = leftover.astype(jnp.bfloat16)
    return (input_grads[None], new_momentum[None], new_worker[None, None], new_server[None])


def solution(mesh):
    return jax.shard_map(
        body,
        mesh=mesh,
        in_specs=(
            P("pipe", None, "rep", None),
            P("pipe", "rep", None),
            P("rep", None),
            P("pipe", None, None),
            P("pipe", None, None),
            P("pipe", None, None, None),
            P("pipe", "rep", None, None, None),
            P("pipe", None, None, "rep"),
        ),
        out_specs=(
            P("pipe", "rep", None),
            P("pipe", None, None, None),
            P("pipe", "rep", None, None, None),
            P("pipe", None, None, "rep"),
        ),
        check_vma=False,
    )
```

profile of v0, /device:TPU:1, one launch (start us, length us, event | category | flops | bytes accessed | tf_op | source)
XLA Modules:
  0.0 298.3 jit_solution(619635839344201911)
XLA Ops:
  8.7 4.1 %fusion.14 = f32[128,64]{0,1:T(8,128)S(1)} fusion(bf16[1,2,128,14336]{3,2,1,0:T(8,128)(2,1)} %param.8, bf16[1,64,14336]{2,1,0:T(8,128)(2,1)S(1)} %copy-done), kind=kOutput, calls=%fused_computation.30 | convolution fusion | flops 234881024 | bytes 5537792 | tf_op jit(solution)/shard_map/td,kd->tk/dot_general | solution.py:41
  21.4 4.3 %copy.63 = f32[16,8,112,128]{3,2,1,0:T(8,128)} copy(f32[16,8,112,128]{3,1,2,0:T(8,128)S(1)} %bitcast.132) | data formatting | bytes 14680064
  26.5 4.2 %copy.60 = f32[16,8,112,128]{3,2,1,0:T(8,128)} copy(f32[16,8,112,128]{3,1,2,0:T(8,128)S(1)} %bitcast.134) | data formatting | bytes 14680064
  30.7 4.3 %copy.67 = f32[16,8,16,896]{3,2,1,0:T(8,128)} copy(f32[16,8,16,896]{3,1,2,0:T(8,128)S(1)} %bitcast.133) | data formatting | bytes 14680064
  35.0 4.3 %copy.64 = f32[16,8,16,896]{3,2,1,0:T(8,128)} copy(f32[16,8,16,896]{3,1,2,0:T(8,128)S(1)} %bitcast.135) | data formatting | bytes 14680064
  39.2 3.4 %fusion.10 = f32[128,64]{0,1:T(8,128)S(1)} fusion(bf16[1,2,128,14336]{3,2,1,0:T(8,128)(2,1)} %param.8, bf16[1,64,14336]{2,1,0:T(8,128)(2,1)S(1)} %copy-done), kind=kOutput, calls=%fused_computation.26 | convolution fusion | flops 234881024 | bytes 5537792 | tf_op jit(solution)/shard_map/td,kd->tk/dot_general | solution.py:41
  46.5 54.4 %collective-permute-done = bf16[128,14336]{1,0:T(8,128)(2,1)} collective-permute-done((bf16[128,14336]{1,0:T(8,128)(2,1)}, bf16[128,14336]{1,0:T(8,128)(2,1)}, u32[]{:S(2)}, u32[]{:S(2)}) %collective-permute-start) | collective-permute-done | bytes 3670048 | tf_op jit(solution)/shard_map/ppermute | solution.py:17
  107.2 3.5 %convolution_add_fusion = f32[64,14336]{1,0:T(8,128)S(1)} fusion(f32[64,14336]{1,0:T(8,128)S(1)} %fusion.16, bf16[128,14336]{1,0:T(8,128)(2,1)S(1)} %copy-done.8, bf16[128,14336]{1,0:T(8,128)(2,1)} %collective-permute-done, pred[]{:T(512)S(6)} %eq.3, f32[128,64]{0,1:T(8,128)S(1)} %fusion.10), kind=kOutput, calls=%fused_computation.2 | convolution fusion | flops 237707264 | bytes 14712833 | tf_op jit(solution)/shard_map/tk,td->kd/dot_general | solution.py:48
  116.9 4.3 %div.58 = f32[2,64,112,128]{3,2,1,0:T(8,128)} broadcast(bf16[2,64,112]{2,1,0:T(8,128)(2,1)S(1)} %add_convert_fusion), dimensions={0,1,2} | broadcast | bytes 7368704 | tf_op jit(solution)/shard_map/div | solution.py:35
  121.2 9.1 %div.59 = f32[2,64,16,896]{3,2,1,0:T(8,128)} reshape(f32[2,64,112,128]{3,2,1,0:T(8,128)} %div.58) | data formatting | bytes 14680064 | tf_op jit(solution)/shard_map/div | solution.py:35
  130.3 4.7 %copy.65 = f32[8,8,16,896]{3,2,1,0:T(8,128)} copy(f32[8,8,16,896]{3,1,2,0:T(8,128)} %bitcast.140) | data formatting | bytes 7340032
  138.1 8.7 %all-to-all-start = ((bf16[16,2,448]{2,1,0:T(2,128)(2,1)}), bf16[16,2,448]{2,1,0:T(2,128)(2,1)S(1)}, u32[]{:S(2)}, u32[]{:S(2)}) async-start(bf16[16,2,448]{2,1,0:T(2,128)(2,1)} %reshape.168), calls=%async_computation | async-start | bytes 65536 | tf_op jit(solution)/shard_map/all_to_all | solution.py:107
  146.8 10.5 %fusion.3 = bf16[2,64,16,896]{3,2,1,0:T(8,128)(2,1)S(1)} fusion(f32[2,64,16,896]{3,2,1,0:T(8,128)} %div.59, f32[1,64,16,896]{3,2,1,0:T(8,128)} %bitcast.151, f32[1,64,16,896]{3,2,1,0:T(8,128)} %bitcast.150, f32[2,64,16,896]{3,2,1,0:T(8,128)} %bitcast.142, f32[2,64,16,896]{3,2,1,0:T(8,128)} %bitcast.143), kind=kLoop, calls=%fused_computation.8 | loop fusion | flops 12845056 | bytes 33030144 | tf_op jit(solution)/shard_map/convert_element_type | solution.py:35
  160.0 7.4 %all-to-all-start.1 = ((bf16[2,64,16,896]{3,1,0,2:T(8,128)(2,1)}), bf16[2,64,16,896]{3,1,0,2:T(8,128)(2,1)}, u32[]{:S(2)}, u32[]{:S(2)}) async-start(bf16[2,64,16,896]{3,1,0,2:T(8,128)(2,1)} %copy.55), calls=%async_computation.1 | async-start | bytes 7340032 | tf_op jit(solution)/shard_map/all_to_all | solution.py:106
  168.4 4.7 %mul.214 = f32[2,64,16,7,128]{4,3,2,1,0:T(8,128)} broadcast(f32[2,64,16,7]{3,2,1,0:T(8,128)S(1)} %copy.54), dimensions={0,1,2,3} | broadcast | bytes 7397376 | tf_op jit(solution)/shard_map/mul | solution.py:62
  173.1 9.3 %mul.215 = f32[2,64,16,896]{3,2,1,0:T(8,128)} reshape(f32[2,64,16,7,128]{4,3,2,1,0:T(8,128)} %mul.214) | data formatting | bytes 14680064 | tf_op jit(solution)/shard_map/mul | solution.py:62
  182.3 33.7 %all-to-all-done.1 = bf16[2,64,16,896]{3,1,0,2:T(8,128)(2,1)} async-done(((bf16[2,64,16,896]{3,1,0,2:T(8,128)(2,1)}), bf16[2,64,16,896]{3,1,0,2:T(8,128)(2,1)}, u32[]{:S(2)}, u32[]{:S(2)}) %all-to-all-start.1) | async-done | bytes 3670048 | tf_op jit(solution)/shard_map/all_to_all | solution.py:106
  216.1 7.4 %multiply_reduce_fusion = f32[2,64,896]{2,1,0:T(8,128)S(1)} fusion(f32[2,64,16,896]{3,2,1,0:T(8,128)} %mul.215, bf16[2,64,16,896]{3,1,0,2:T(8,128)(2,1)} %all-to-all-done.1), kind=kLoop, calls=%fused_computation.22 | loop fusion | flops 5390336 | bytes 11468800 | tf_op jit(solution)/shard_map/reduce_sum | solution.py:65
  227.8 8.1 %div.69 = f32[1,1,2,64,14336]{4,3,2,1,0:T(8,128)} reshape(f32[2,64,112,128]{3,2,1,0:T(8,128)} %div.58) | data formatting | bytes 14680064 | tf_op jit(solution)/shard_map/div | solution.py:35
  238.8 9.7 %subtract_convert_fusion = bf16[1,1,2,64,14336]{4,3,2,1,0:T(8,128)(2,1)} fusion(f32[1,1,2,64,14336]{4,3,2,1,0:T(8,128)} %div.69, f32[1,1,1,64,14336]{4,3,2,1,0:T(8,128)S(1)} %bitcast.138, f32[1,1,1,64,14336]{4,3,2,1,0:T(8,128)} %bitcast.141, bf16[1,1,2,64,14336]{4,3,2,1,0:T(8,128)(2,1)} %param.14, bf16[1,2,64,14336]{3,2,1,0:T(8,128)(2,1)} %param.13), kind=kLoop, calls=%fused_computation.19 | loop fusion | flops 25690112 | bytes 25690112 | tf_op jit(solution)/shard_map/convert_element_type | solution.py:117
  248.6 22.9 %all_gather.6 = bf16[2,64,112]{1,0,2:T(2,128)(2,1)S(1)} all-gather(bf16[2,64,7]{1,0,2:T(2,128)(2,1)S(1)} %add_convert_fusion.1), channel_id=1, replica_groups=mesh['pipe'=8,'rep'=16] {'rep'}, dimensions={2}, use_global_device_ids=true | all-gather | bytes 30464 | tf_op jit(solution)/shard_map/all_gather | solution.py:114
  271.6 4.2 %mul.220 = f32[2,64,112,128]{3,2,1,0:T(8,128)} broadcast(bf16[2,64,112]{2,1,0:T(8,128)(2,1)S(1)} %copy.58), dimensions={0,1,2} | broadcast | bytes 7368704 | tf_op jit(solution)/shard_map/mul | solution.py:74
  275.8 8.1 %mul.221 = f32[2,64,14336]{2,1,0:T(8,128)} reshape(f32[2,64,112,128]{3,2,1,0:T(8,128)} %mul.220) | data formatting | bytes 14680064 | tf_op jit(solution)/shard_map/mul | solution.py:74
  284.7 6.7 %fusion.8 = bf16[1,2,64,14336]{3,2,1,0:T(8,128)(2,1)} fusion(f32[2,64,14336]{2,1,0:T(8,128)} %mul.221, bf16[2,64,14336]{2,1,0:T(8,128)(2,1)} %all-gather.2.cloned.1.call-done), kind=kLoop, calls=%fused_computation.24 | loop fusion | flops 5505024 | bytes 14680064 | tf_op jit(solution)/shard_map/broadcast_in_dim | solution.py:118
  (79 shorter events, 42.3 us)
Async XLA Ops:
  7.2 1.5 copy-start
  7.2 5.6 %copy-start.11 = (bf16[1,64,14336]{2,1,0:T(8,128)(2,1)S(1)}, bf16[1,64,14336]{2,1,0:T(8,128)(2,1)}, u32[]{:S(2)}) copy-start(bf16[1,64,14336]{2,1,0:T(8,128)(2,1)} %param.12) | copy-start | bytes 5505028
  7.2 5.6 %copy-start.5 = (bf16[1,128,14336]{2,1,0:T(8,128)(2,1)S(1)}, bf16[1,128,14336]{2,1,0:T(8,128)(2,1)}, u32[]{:S(2)}) copy-start(bf16[1,128,14336]{2,1,0:T(8,128)(2,1)} %param.9) | copy-start | bytes 11010052
  17.1 83.7 %collective-permute-start = (bf16[128,14336]{1,0:T(8,128)(2,1)}, bf16[128,14336]{1,0:T(8,128)(2,1)}, u32[]{:S(2)}, u32[]{:S(2)}) collective-permute-start(bf16[128,14336]{1,0:T(8,128)(2,1)} %convolution_convert_fusion.1), channel_id=1, source_target_pairs={{16,0},{32,16},{48,32},{64,48},{80,64},{96,80},{112,96},{17,1},{33... | collective-permute-start | bytes 11010056 | tf_op jit(solution)/shard_map/ppermute | solution.py:17
  21.4 4.3 %copy-start.7 = (bf16[1,2,64,14336]{3,2,1,0:T(8,128)(2,1)S(1)}, bf16[1,2,64,14336]{3,2,1,0:T(8,128)(2,1)}, u32[]{:S(2)}) copy-start(bf16[1,2,64,14336]{3,2,1,0:T(8,128)(2,1)} %param.13) | copy-start | bytes 11010052
  42.7 3.1 %copy-start.6 = (bf16[1,128,14336]{2,1,0:T(8,128)(2,1)S(1)}, bf16[1,128,14336]{2,1,0:T(8,128)(2,1)}, u32[]{:S(2)}) copy-start(bf16[1,128,14336]{2,1,0:T(8,128)(2,1)} %param.9) | copy-start | bytes 11010052
  42.7 58.2 %copy-start.8 = (bf16[128,14336]{1,0:T(8,128)(2,1)S(1)}, bf16[128,14336]{1,0:T(8,128)(2,1)}, u32[]{:S(2)}) copy-start(bf16[128,14336]{1,0:T(8,128)(2,1)} %param.10) | copy-start | bytes 11010052
  45.8 55.1 %copy-start.12 = (bf16[1,64,14336]{2,1,0:T(8,128)(2,1)S(1)}, bf16[1,64,14336]{2,1,0:T(8,128)(2,1)}, u32[]{:S(2)}) copy-start(bf16[1,64,14336]{2,1,0:T(8,128)(2,1)} %param.12) | copy-start | bytes 5505028
  45.8 58.3 %slice-start.4 = ((s8[7340032]{0:T(1024)(128)(4,1)}), s8[4194304]{0:T(1024)(128)(4,1)S(1)}, s32[]{:S(2)}) async-start(s8[7340032]{0:T(1024)(128)(4,1)} %bitcast.154), calls=%async_computation.7 | async-start | bytes 8388608
  46.5 57.6 %slice-start.5 = ((s8[7340032]{0:T(1024)(128)(4,1)}), s8[3145728]{0:T(1024)(128)(4,1)S(1)}, s32[]{:S(2)}) async-start(s8[7340032]{0:T(1024)(128)(4,1)} %bitcast.154), calls=%async_computation.8 | async-start | bytes 6291456
  104.8 1.8 copy-start.4
  106.5 6.0 %slice-start = ((s8[7340032]{0:T(1024)(128)(4,1)}), s8[4194304]{0:T(1024)(128)(4,1)S(1)}, s32[]{:S(2)}) async-start(s8[7340032]{0:T(1024)(128)(4,1)} %bitcast.144), calls=%async_computation.3 | async-start | bytes 8388608
  106.5 6.0 %slice-start.2 = ((s8[7340032]{0:T(1024)(128)(4,1)}), s8[4194304]{0:T(1024)(128)(4,1)S(1)}, s32[]{:S(2)}) async-start(s8[7340032]{0:T(1024)(128)(4,1)} %bitcast.147), calls=%async_computation.5 | async-start | bytes 8388608
  107.2 5.6 %slice-start.1 = ((s8[7340032]{0:T(1024)(128)(4,1)}), s8[3145728]{0:T(1024)(128)(4,1)S(1)}, s32[]{:S(2)}) async-start(s8[7340032]{0:T(1024)(128)(4,1)} %bitcast.144), calls=%async_computation.4 | async-start | bytes 6291456
  107.2 7.2 %slice-start.3 = ((s8[7340032]{0:T(1024)(128)(4,1)}), s8[3145728]{0:T(1024)(128)(4,1)S(1)}, s32[]{:S(2)}) async-start(s8[7340032]{0:T(1024)(128)(4,1)} %bitcast.147), calls=%async_computation.6 | async-start | bytes 6291456
  110.7 1.9 copy-start.1
  130.3 4.7 %copy-start.2 = (f32[64,14336]{1,0:T(8,128)S(1)}, f32[64,14336]{1,0:T(8,128)}, u32[]{:S(2)}) copy-start(f32[64,14336]{1,0:T(8,128)} %copy-done.1) | copy-start | bytes 11010052
  138.1 21.9 %all-to-all-start = ((bf16[16,2,448]{2,1,0:T(2,128)(2,1)}), bf16[16,2,448]{2,1,0:T(2,128)(2,1)S(1)}, u32[]{:S(2)}, u32[]{:S(2)}) async-start(bf16[16,2,448]{2,1,0:T(2,128)(2,1)} %reshape.168), calls=%async_computation | async-start | bytes 65536 | tf_op jit(solution)/shard_map/all_to_all | solution.py:107
  160.0 7.4 %copy-start.9 = (bf16[1,2,64,896]{3,2,1,0:T(8,128)(2,1)S(1)}, bf16[1,2,64,896]{3,2,1,0:T(8,128)(2,1)}, u32[]{:S(2)}) copy-start(bf16[1,2,64,896]{3,2,1,0:T(8,128)(2,1)} %param.15) | copy-start | bytes 688132
  160.0 56.1 %all-to-all-start.1 = ((bf16[2,64,16,896]{3,1,0,2:T(8,128)(2,1)}), bf16[2,64,16,896]{3,1,0,2:T(8,128)(2,1)}, u32[]{:S(2)}, u32[]{:S(2)}) async-start(bf16[2,64,16,896]{3,1,0,2:T(8,128)(2,1)} %copy.55), calls=%async_computation.1 | async-start | bytes 7340032 | tf_op jit(solution)/shard_map/all_to_all | solution.py:106
  167.4 117.4 %all-gather.2.cloned.1.call-start = ((), (), s32[]{:S(2)}) async-start(), calls=%async_computation.2 | async-start | bytes 3899392 | tf_op jit(solution)/shard_map/all_gather | solution.py:113
  235.9 3.0 copy-start.3
  275.8 8.1 %copy-start.10 = (bf16[1,2,64,896]{3,2,1,0:T(8,128)(2,1)S(1)}, bf16[1,2,64,896]{3,2,1,0:T(8,128)(2,1)}, u32[]{:S(2)}) copy-start(bf16[1,2,64,896]{3,2,1,0:T(8,128)(2,1)} %param.15) | copy-start | bytes 688132
Sparse Core Ops, SparseCore 0:
  227.9 55.8 all-gather.1
where the time goes:
time: 299 us; the launch traced here: 298 us
  waiting for transfers between devices  88.2 us (29%)
  local copies, waits for them, and re-layouts  86 us (29%)
  other arithmetic  43.8 us (15%)
  matrix products  25.6 us (9%)
  blocking collectives  22.9 us (8%)
  starting transfers between devices  17.5 us (6%)
  between operations  14.4 us (5%)
    ppermute x1, waiting for transfers between devices, passed_along(): lax.ppermute(value, axis, [(source, source + steps) for source in range(i...  54.4 us
    all_to_all x1, waiting for transfers between devices, body(): lax.all_to_all(block_levels, 'rep', split_axis=2, concat_axis=2, tiled=True)  33.7 us
    unnamed x48, local copies, waits for them, and re-layouts  32.9 us
    all_gather x1, blocking collectives, body(): lax.all_gather(server_scales, 'rep', axis=2, tiled=True)  22.9 us
    div x6, local copies, waits for them, and re-layouts, compress(): levels = jnp.clip(grouped / widened, -1.0, 1.0).astype(jnp.bfloat16)  21.8 us
    mul x2, local copies, waits for them, and re-layouts, serve_blocks(): received_scales.astype(jnp.float32)[..., None]  14 us
    mul x2, local copies, waits for them, and re-layouts, restore(): scales.astype(jnp.float32)[..., None]  12.3 us
    convert_element_type x2, other arithmetic, compress(): levels = jnp.clip(grouped / widened, -1.0, 1.0).astype(jnp.bfloat16)  12.2 us
  transfers between devices with their start and end apart: 4, of which 2 were waited for; matrix products, arithmetic and copies ran while one was open for 30% of the time, Pallas kernels for 0%

commit v1 on v0

v1 whole, which is shorter than its diff:
```python
import jax
import jax.numpy as jnp
from jax import lax
from jax.experimental import pallas as pl
from jax.experimental.pallas import tpu as pltpu
from jax.sharding import PartitionSpec as P

GRP = 128
D = 14336
K = 64
TOK = 128
BLK = 896
QTR = 3584
PIECE = 1792
GROUPS = BLK // GRP

MOMENTUM_DECAY = 0.9
EPSILON = 1e-06
GELU_ROOT = 0.7978845608028654

MESH = pl.DeviceIdType.MESH
OFFSETS = (2, 1, 3, 0)
F32 = jnp.float32
BF16 = jnp.bfloat16


def nt_dot(left, right):
    return lax.dot_general(left, right, (((1,), (1,)), ((), ())), preferred_element_type=F32)


def nn_dot(left, right):
    return lax.dot_general(left, right, (((1,), (0,)), ((), ())), preferred_element_type=F32)


def gelu_parts(hidden):
    argument = GELU_ROOT * (hidden + 0.044715 * hidden * hidden * hidden)
    tangent = jnp.tanh(argument)
    gelu_value = 0.5 * hidden * (1.0 + tangent)
    gelu_slope = 0.5 * (1.0 + tangent) + 0.5 * hidden * (1.0 - tangent * tangent) * GELU_ROOT * (
        1.0 + 3.0 * 0.044715 * hidden * hidden
    )
    return gelu_value, gelu_slope


def compress_group(values):
    mean = jnp.sum(jnp.abs(values), axis=1, keepdims=True) * (1.0 / GRP)
    scale = (mean + EPSILON).astype(BF16).astype(F32)
    level = jnp.clip(values * (1.0 / scale), -1.0, 1.0).astype(BF16).astype(F32)
    return scale * level


def kernel(
    acts, ups, fin, w_in, w_out, mom, err, serr,
    ig, nm, nw, ns,
    src, win_v, wout_v, wnx_v, mom_v, err_v, serr_v, nw_v, ig_v, nm_v, ns_v,
    v_sib, v_own, r_sib, x1, x2, z1, z2,
    slope_v, factor, hg_out, hg_next,
    l_a, l_w, l_u, l_o, l_misc, o_sem, nm_sem,
    wa_s, wa_r, wb_s, wb_r, wc_s, wc_r, hg_s, hg_r,
    sib_s, sib_r, x1_s, x1_r, x2_s, x2_r, z1_s, z1_r, z2_s, z2_r,
    gx_s, gx_r, gz_s, gz_r, gs_s, gs_r, hx_s, hx_r, hz_s, hz_r, ts_s, ts_r,
):
    p = lax.axis_index("pipe")
    r = lax.axis_index("rep")
    zh = r // 8
    x = lax.rem(r // 2, 4)
    c = lax.rem(r, 2)

    def at(zh_, x_, c_):
        return (p, zh_ * 8 + x_ * 2 + c_)

    def x_of(offset):
        return lax.rem(x + offset, 4)

    sibling = at(zh, x, 1 - c)
    partner = at(1 - zh, x, c)
    x_peer = [at(zh, x_of(o), c) for o in OFFSETS[:3]]
    prev = (lax.rem(p + 7, 8), r)
    nxt = (lax.rem(p + 1, 8), r)
    is_last = p == 7

    def cols(start, size):
        return pl.ds(pl.multiple_of(start, GRP), size)

    loads_a, loads_w, loads_u, loads_o = [], [], [], []
    for q in range(4):
        s = pl.ds(q * QTR, QTR)
        loads_a.append(pltpu.make_async_copy(acts.at[0, :, :, s], src.at[0, :, :, s], l_a.at[q]))
        loads_w.append(pltpu.make_async_copy(w_in.at[0, :, s], win_v.at[:, s], l_w.at[q]))
        loads_u.append(pltpu.make_async_copy(ups.at[0, :, s], src.at[1, 0, :, s], l_u.at[q]))
        loads_o.append(pltpu.make_async_copy(w_out.at[0, :, s], wout_v.at[:, s], l_o.at[q]))
    load_mom = pltpu.make_async_copy(mom.at[0], mom_v, l_misc.at[0])
    load_err = pltpu.make_async_copy(err.at[0, 0], err_v, l_misc.at[1])
    load_serr = pltpu.make_async_copy(serr.at[0], serr_v, l_misc.at[2])
    load_fin = pltpu.make_async_copy(fin, src.at[1, 1], l_misc.at[3])
    for q in range(4):
        loads_w[q].start()
        loads_a[q].start()
    for q in range(4):
        loads_o[q].start()
        loads_u[q].start()
    load_mom.start()
    load_err.start()
    load_serr.start()

    @pl.when(is_last)
    def _():
        load_fin.start()

    barrier = pltpu.get_barrier_semaphore()
    for device in [sibling, partner, nxt] + x_peer:
        pl.semaphore_signal(barrier, inc=1, device_id=device, device_id_type=MESH)
    pl.semaphore_wait(barrier, 6)

    sent = []

    def send(source, target, s_sem, r_sem, device):
        copy = pltpu.make_async_remote_copy(
            src_ref=source, dst_ref=target, send_sem=s_sem, recv_sem=r_sem, device_id=device, device_id_type=MESH
        )
        copy.start()
        sent.append(copy)
        return copy

    def piece(offset, core):
        return cols((x_of(offset) * 2 + core) * PIECE, PIECE)

    wa = [
        send(w_in.at[0, :, piece(o, c)], wnx_v.at[:, piece(o, c)], wa_s.at[i], wa_r.at[i], prev)
        for i, o in enumerate((0, 2))
    ]

    hidden = jnp.zeros((K, 2 * TOK), F32)
    for q in range(4):
        loads_w[q].wait()
        loads_a[q].wait()
        s = pl.ds(q * QTR, QTR)
        hidden = hidden + nt_dot(win_v[:, s], src[0, :, :, s].reshape(2 * TOK, QTR))
    gelu_value, gelu_slope = gelu_parts(hidden)
    factor[1] = gelu_value.astype(BF16)
    slope_v[...] = gelu_slope

    wc = []

    def to_sibling(i, offset):
        wc.append(send(wnx_v.at[:, piece(offset, c)], wnx_v.at[:, piece(offset, c)], wc_s.at[i], wc_r.at[i], sibling))

    wa[0].wait_recv()
    wb = [
        send(wnx_v.at[:, piece(0, c)], wnx_v.at[:, piece(0, c)], wb_s.at[i], wb_r.at[i], at(zh, x_of(o), c))
        for i, o in enumerate((1, 3))
    ]
    to_sibling(0, 0)

    up = jnp.zeros((K, TOK), F32)
    for q in range(4):
        loads_o[q].wait()
        loads_u[q].wait()
        s = pl.ds(q * QTR, QTR)
        up = up + nt_dot(wout_v[:, s], src[1, 0, :, s])
    hg = (up * slope_v[:, :TOK]).astype(BF16)
    factor[0, :, :TOK] = hg
    hg_out[...] = hg
    hg_copy = send(hg_out, hg_next, hg_s, hg_r, prev)

    wa[1].wait_recv()
    to_sibling(1, 2)
    wb[0].wait_recv()
    to_sibling(2, 3)
    wb[1].wait_recv()
    to_sibling(3, 1)
    for copy in wc:
        copy.wait_recv()
    hg_copy.wait_recv()

    @pl.when(jnp.logical_not(is_last))
    def _():
        left = hg_next[...].astype(F32).T.astype(BF16)

        def step(t, carry):
            s = cols(t * BLK, BLK)
            src[1, 1, :, s] = nn_dot(left, wnx_v[:, s]).astype(BF16)
            return carry

        lax.fori_loop(0, D // BLK, step, 0)

    @pl.when(is_last)
    def _():
        load_fin.wait()

    up = jnp.zeros((K, TOK), F32)
    for q in range(4):
        s = pl.ds(q * QTR, QTR)
        up = up + nt_dot(wout_v[:, s], src[1, 1, :, s])
    hg1 = up * slope_v[:, TOK:]
    factor[0, :, TOK:] = hg1.astype(BF16)

    load_mom.wait()
    load_err.wait()

    def half(k, core, target):
        x_to = x_of(OFFSETS[k])

        def step(i, carry):
            mat = i // 2
            zz = lax.rem(i, 2)
            base = (zz * 8 + x_to * 2 + core) * BLK
            block = cols(base, BLK)
            grad = nn_dot(factor[mat], src[mat, :, :, block].reshape(2 * TOK, BLK))
            for g in range(GROUPS):
                s = cols(base + g * GRP, GRP)
                blended = (
                    MOMENTUM_DECAY * mom_v[mat, :, s].astype(F32)
                    + (1.0 - MOMENTUM_DECAY) * grad[:, g * GRP : (g + 1) * GRP]
                    + err_v[mat, :, s].astype(F32)
                )
                value = compress_group(blended)
                nw_v[mat, :, s] = (blended - value).astype(BF16)
                target[k, mat, zz, :, g * GRP : (g + 1) * GRP] = value.astype(BF16)
            return carry

        lax.fori_loop(0, 4, step, 0)

    sib = []
    x1c, z1c = [], []

    def pair(k):
        sib[k].wait_recv()

        def step(i, carry):
            mat = i // 2
            zz = lax.rem(i, 2)
            v_own[k, mat, zz] = (v_own[k, mat, zz].astype(F32) + r_sib[k, mat, zz].astype(F32)).astype(BF16)
            return carry

        lax.fori_loop(0, 4, step, 0)
        z1c.append(send(v_own.at[k, 1, 1 - zh], z1.at[k], z1_s.at[k], z1_r.at[k], partner))
        if k < 3:
            x1c.append(send(v_own.at[k, 0], x1.at[k], x1_s.at[k], x1_r.at[k], x_peer[k]))

    for k in range(4):
        half(k, 1 - c, v_sib)
        sib.append(send(v_sib.at[k], r_sib.at[k], sib_s.at[k], sib_r.at[k], sibling))
        if k > 0:
            pair(k - 1)
        half(k, c, v_own)
    pair(3)
    store_nw = pltpu.make_async_copy(nw_v, nw.at[0, 0], o_sem.at[0])
    store_nw.start()

    z2c = []
    for k in range(3):
        z1c[k].wait_recv()
        v_own[k, 1, zh] = (v_own[k, 1, zh].astype(F32) + z1[k].astype(F32)).astype(BF16)
        z2c.append(send(v_own.at[k, 1, zh], z2.at[k], z2_s.at[k], z2_r.at[k], x_peer[k]))

    left = hg1.T.astype(BF16)

    def ig_step(t, carry):
        s = cols(t * BLK, BLK)
        ig_v[:, s] = nn_dot(left, win_v[:, s]).astype(BF16)
        return carry

    lax.fori_loop(0, D // BLK, ig_step, 0)
    store_ig = pltpu.make_async_copy(ig_v, ig.at[0], o_sem.at[1])
    store_ig.start()
    load_serr.wait()

    for k in range(3):
        x1c[k].wait_recv()
    other = 1 - zh
    v_own[3, 0, other] = (
        v_own[3, 0, other].astype(F32)
        + x1[0, other].astype(F32)
        + x1[1, other].astype(F32)
        + x1[2, other].astype(F32)
    ).astype(BF16)
    x2c = send(v_own.at[3, 0, other], x2, x2_s, x2_r, partner)

    my_cols = r * BLK

    def serve(mat, terms):
        for g in range(GROUPS):
            gs = slice(g * GRP, (g + 1) * GRP)
            total = v_own[3, mat, zh, :, gs].astype(F32)
            for term in terms:
                total = total + term[:, gs].astype(F32)
            combined = total * (1.0 / 16.0) + serr_v[mat, :, gs].astype(F32)
            value = compress_group(combined)
            ns_v[mat, :, gs] = (combined - value).astype(BF16)
            nm_v[mat, :, cols(my_cols + g * GRP, GRP)] = value.astype(BF16)

    z1c[3].wait_recv()
    for k in range(3):
        z2c[k].wait_recv()
    serve(1, [z1.at[3], z2.at[0], z2.at[1], z2.at[2]])
    x2c.wait_recv()
    serve(0, [x1.at[0, zh], x1.at[1, zh], x1.at[2, zh], x2])
    store_ns = pltpu.make_async_copy(ns_v, ns.at[0], o_sem.at[2])
    store_ns.start()

    def block_of(ref, zh_, x_, c_, mat=None):
        s = cols((zh_ * 8 + x_ * 2 + c_) * BLK, BLK)
        return ref.at[:, :, s] if mat is None else ref.at[mat, :, s]

    stored = []

    def store(zh_, x_, c_, mat=None):
        copy = pltpu.make_async_copy(
            block_of(nm_v, zh_, x_, c_, mat), block_of(nm.at[0], zh_, x_, c_, mat), nm_sem.at[len(stored)]
        )
        copy.start()
        stored.append(copy)

    def push(zh_, x_, mat, s_sem, r_sem, device):
        b = block_of(nm_v, zh_, x_, c, mat)
        return send(b, b, s_sem, r_sem, device)

    sibs = []

    def share(zh_, x_, mat):
        i = len(sibs)
        sibs.append((push(zh_, x_, mat, gs_s.at[i], gs_r.at[i], sibling), zh_, x_, mat))
        store(zh_, x_, c, mat)

    gx = [push(zh, x, None, gx_s.at[k], gx_r.at[k], x_peer[k]) for k in range(3)]
    gz = push(zh, x, None, gz_s, gz_r, partner)
    share(zh, x, None)
    gz.wait_recv()
    hx = [push(other, x, 0, hx_s.at[k], hx_r.at[k], x_peer[k]) for k in range(3)]
    share(other, x, None)
    hz = [None] * 3
    for k in (1, 2, 0):
        gx[k].wait_recv()
        x_from = x_of(4 - OFFSETS[k])
        hz[k] = push(zh, x_from, 1, hz_s.at[k], hz_r.at[k], partner)
        share(zh, x_from, None)
    for k in (1, 2, 0):
        x_from = x_of(4 - OFFSETS[k])
        hx[k].wait_recv()
        share(other, x_from, 0)
        hz[k].wait_recv()
        share(other, x_from, 1)
    for copy, zh_, x_, mat in sibs:
        copy.wait_recv()
        store(zh_, x_, 1 - c, mat)

    for copy in sent:
        copy.wait_send()
    for copy in stored:
        copy.wait()
    store_nw.wait()
    store_ig.wait()
    store_ns.wait()


def body(*arrays):
    dma = pltpu.SemaphoreType.DMA
    vmem = pltpu.VMEM
    return pl.pallas_call(
        kernel,
        name="cascade",
        out_shape=(
            jax.ShapeDtypeStruct((1, TOK, D), BF16),
            jax.ShapeDtypeStruct((1, 2, K, D), BF16),
            jax.ShapeDtypeStruct((1, 1, 2, K, D), BF16),
            jax.ShapeDtypeStruct((1, 2, K, BLK), BF16),
        ),
        in_specs=[pl.BlockSpec(memory_space=pl.ANY)] * 8,
        out_specs=(pl.BlockSpec(memory_space=pl.ANY),) * 4,
        scratch_shapes=[
            vmem((2, 2, TOK, D), BF16),
            vmem((K, D), BF16),
            vmem((K, D), BF16),
            vmem((K, D), BF16),
            vmem((2, K, D), BF16),
            vmem((2, K, D), BF16),
            vmem((2, K, BLK), BF16),
            vmem((2, K, D), BF16),
            vmem((TOK, D), BF16),
            vmem((2, K, D), BF16),
            vmem((2, K, BLK), BF16),
            vmem((4, 2, 2, K, BLK), BF16),
            vmem((4, 2, 2, K, BLK), BF16),
            vmem((4, 2, 2, K, BLK), BF16),
            vmem((3, 2, K, BLK), BF16),
            vmem((K, BLK), BF16),
            vmem((4, K, BLK), BF16),
            vmem((3, K, BLK), BF16),
            vmem((K, 2 * TOK), F32),
            vmem((2, K, 2 * TOK), BF16),
            vmem((K, TOK), BF16),
            vmem((K, TOK), BF16),
            dma((4,)), dma((4,)), dma((4,)), dma((4,)), dma((4,)), dma((3,)), dma((22,)),
            dma((2,)), dma((2,)), dma((2,)), dma((2,)), dma((4,)), dma((4,)), dma, dma,
            dma((4,)), dma((4,)), dma((3,)), dma((3,)), dma, dma, dma((4,)), dma((4,)), dma((3,)), dma((3,)),
            dma((3,)), dma((3,)), dma, dma, dma((11,)), dma((11,)), dma((3,)), dma((3,)), dma((3,)), dma((3,)),
            dma, dma,
        ],
        compiler_params=pltpu.CompilerParams(
            collective_id=0, has_side_effects=True, vmem_limit_bytes=56 * 2**20
        ),
        cost_estimate=pl.CostEstimate(flops=2_500_000_000, bytes_accessed=37_000_000, transcendentals=20_000),
    )(*arrays)


def solution(mesh):
    return jax.shard_map(
        body,
        mesh=mesh,
        in_specs=(
            P("pipe", None, "rep", None),
            P("pipe", "rep", None),
            P("rep", None),
            P("pipe", None, None),
            P("pipe", None, None),
            P("pipe", None, None, None),
            P("pipe", "rep", None, None, None),
            P("pipe", None, None, "rep"),
        ),
        out_specs=(
            P("pipe", "rep", None),
            P("pipe", None, None, None),
            P("pipe", "rep", None, None, None),
            P("pipe", None, None, "rep"),
        ),
        check_vma=False,
    )
```

time: 299 us -> 86.7 us (0.29)
  waiting for transfers between devices: 88.2 us -> 0 us
  local copies, waits for them, and re-layouts: 86 us -> 10.2 us
  Pallas kernels: 0 us -> 74.3 us
  other arithmetic: 43.8 us -> 0 us
  matrix products: 25.6 us -> 0 us
  blocking collectives: 22.9 us -> 0 us
  starting transfers between devices: 17.5 us -> 0 us
  between operations: 14.4 us -> 0.65 us
    pallas_call x0 -> x1, Pallas kernels: none -> 74.3 us  [body(): pl.pallas_call(kernel, name='cascade', out_shape=(jax.ShapeDtypeStruct((1...]
    ppermute x1 -> x0, waiting for transfers between devices: 54.4 us -> none  [passed_along(): lax.ppermute(value, axis, [(source, source + steps) for source in range(i...]
    all_to_all x2 -> x0, waiting for transfers between devices: 33.7 us -> none  [the longest x1 33.7 us: body(): lax.all_to_all(block_levels, 'rep', split_axis=2, concat_axis=2, tiled=True)]
    mul x4 -> x0, local copies, waits for them, and re-layouts: 26.3 us -> none  [the longest x2 14 us: serve_blocks(): received_scales.astype(jnp.float32)[..., None]]
    dot_general x10 -> x0, matrix products: 25.6 us -> none  [the longest x4 7.62 us: outer_sum(): jnp.einsum('tk,td->kd', left, right, preferred_element_type=jnp.float32)]
    convert_element_type x8 -> x0, other arithmetic: 25.5 us -> none  [the longest x2 12.2 us: compress(): levels = jnp.clip(grouped / widened, -1.0, 1.0).astype(jnp.bfloat16)]
    div x7 -> x0, local copies, waits for them, and re-layouts: 22.9 us -> none  [the longest x6 21.8 us: compress(): levels = jnp.clip(grouped / widened, -1.0, 1.0).astype(jnp.bfloat16)]
    all_gather x1 -> x0, blocking collectives: 22.9 us -> none  [body(): lax.all_gather(server_scales, 'rep', axis=2, tiled=True)]
  transfers between devices with their start and end apart: 4 -> 0, of which waited for: 2 -> 0; matrix products, arithmetic and copies ran while one was open for 30% -> 0% of each run, Pallas kernels for 0% -> 0%
where the time goes in v1:
time: 86.7 us; the launch traced here: 85.2 us
  Pallas kernels  74.3 us (86%)
  local copies, waits for them, and re-layouts  10.2 us (12%)
    pallas_call x1, Pallas kernels, body(): pl.pallas_call(kernel, name='cascade', out_shape=(jax.ShapeDtypeStruct((1...  74.3 us
    unnamed x10, local copies, waits for them, and re-layouts  10.2 us

profile of v1, /device:TPU:1, one launch (start us, length us, event | category | flops | bytes accessed | tf_op | source)
XLA Modules:
  0.0 85.2 jit_solution(4080777583651938136)
XLA Ops:
  0.6 74.3 %cascade.1 = (bf16[1,128,14336]{2,1,0:T(8,128)(2,1)}, bf16[1,2,64,14336]{3,2,1,0:T(8,128)(2,1)}, bf16[1,1,2,64,14336]{4,3,2,1,0:T(8,128)(2,1)}, bf16[1,2,64,896]{3,2,1,0:T(8,128)(2,1)}) custom-call(bf16[1,2,128,14336]{3,2,1,0:T(8,128)(2,1)} %acts.1, bf16[1,128,14336]{2,1,0:T(8,128)(2,1)} %ups.1, bf16[128,14336]{1,0:T(8,128)(2,1)} %fin.1, ...), custom_call_target="tpu_custom_call" | custom-call | flops 2500000000 | bytes 37000000 | tf_op jit(solution)/shard_map/cascade/pallas_call | solution.py:360
  75.0 0.0 copy-start.1
  75.0 4.3 %copy.16 = bf16[1,128,14336]{2,1,0:T(8,128)(2,1)} copy(bf16[1,128,14336]{2,1,0:T(8,128)(2,1)} %get-tuple-element.8) | data formatting | bytes 7340032
  79.3 0.0 copy-done.1
  79.3 0.0 copy-start
  79.3 1.9 %copy.17 = bf16[1,2,64,14336]{3,2,1,0:T(8,128)(2,1)} copy(bf16[1,2,64,14336]{3,2,1,0:T(8,128)(2,1)S(1)} %copy-done.1) | data formatting | bytes 7340032
  81.2 1.5 %copy-done = bf16[1,1,2,64,14336]{4,3,2,1,0:T(8,128)(2,1)S(1)} copy-done((bf16[1,1,2,64,14336]{4,3,2,1,0:T(8,128)(2,1)S(1)}, bf16[1,1,2,64,14336]{4,3,2,1,0:T(8,128)(2,1)}, u32[]{:S(2)}) %copy-start) | copy-done | bytes 3670040
  82.7 0.0 copy-start.2
  82.7 1.8 %copy.18 = bf16[1,1,2,64,14336]{4,3,2,1,0:T(8,128)(2,1)} copy(bf16[1,1,2,64,14336]{4,3,2,1,0:T(8,128)(2,1)S(1)} %copy-done) | data formatting | bytes 7340032
  84.5 0.0 copy-done.2
  84.5 0.7 copy.19
Async XLA Ops:
  75.0 4.4 %copy-start.1 = (bf16[1,2,64,14336]{3,2,1,0:T(8,128)(2,1)S(1)}, bf16[1,2,64,14336]{3,2,1,0:T(8,128)(2,1)}, u32[]{:S(2)}) copy-start(bf16[1,2,64,14336]{3,2,1,0:T(8,128)(2,1)} %get-tuple-element.9) | copy-start | bytes 11010052
  79.3 3.4 %copy-start = (bf16[1,1,2,64,14336]{4,3,2,1,0:T(8,128)(2,1)S(1)}, bf16[1,1,2,64,14336]{4,3,2,1,0:T(8,128)(2,1)}, u32[]{:S(2)}) copy-start(bf16[1,1,2,64,14336]{4,3,2,1,0:T(8,128)(2,1)} %get-tuple-element.10) | copy-start | bytes 11010052
  82.7 1.8 %copy-start.2 = (bf16[1,2,64,896]{3,2,1,0:T(8,128)(2,1)S(1)}, bf16[1,2,64,896]{3,2,1,0:T(8,128)(2,1)}, u32[]{:S(2)}) copy-start(bf16[1,2,64,896]{3,2,1,0:T(8,128)(2,1)} %get-tuple-element.11) | copy-start | bytes 688132

commit v2 on v1

v2 whole, which is shorter than its diff:
```python
import jax
import jax.numpy as jnp
from jax import lax
from jax.experimental import pallas as pl
from jax.experimental.pallas import tpu as pltpu
from jax.sharding import PartitionSpec as P

GRP = 128
D = 14336
K = 64
TOK = 128
BLK = 896
QTR = 3584
PIECE = 1792
TWO = 2 * BLK
GROUPS = BLK // GRP

MOMENTUM_DECAY = 0.9
EPSILON = 1e-06
GELU_ROOT = 0.7978845608028654

MESH = pl.DeviceIdType.MESH
OFFSETS = (2, 1, 3, 0)
F32 = jnp.float32
BF16 = jnp.bfloat16


def nt_dot(left, right):
    return lax.dot_general(left, right, (((1,), (1,)), ((), ())), preferred_element_type=F32)


def nn_dot(left, right):
    return lax.dot_general(left, right, (((1,), (0,)), ((), ())), preferred_element_type=F32)


def gelu_parts(hidden):
    argument = GELU_ROOT * (hidden + 0.044715 * hidden * hidden * hidden)
    tangent = jnp.tanh(argument)
    gelu_value = 0.5 * hidden * (1.0 + tangent)
    gelu_slope = 0.5 * (1.0 + tangent) + 0.5 * hidden * (1.0 - tangent * tangent) * GELU_ROOT * (
        1.0 + 3.0 * 0.044715 * hidden * hidden
    )
    return gelu_value, gelu_slope


def compress_group(values):
    mean = jnp.sum(jnp.abs(values), axis=1, keepdims=True) * (1.0 / GRP)
    scale = (mean + EPSILON).astype(BF16).astype(F32)
    level = jnp.clip(values * (1.0 / scale), -1.0, 1.0).astype(BF16).astype(F32)
    return scale * level


def kernel(
    acts, ups, fin, w_in, w_out, mom, err, serr,
    ig_v, nm_v, nw_v, ns_v,
    src, win_v, wout_v, wnx_v, mom_v, err_v, serr_v,
    v_own, v_sum, r_sib, x1, x2, z1, z2,
    slope_v, factor, hg_out, hg_next, hg1_v, grad_a, grad_b,
    l_a, l_w, l_u, l_o, l_misc, s_sem, r_sem,
):
    p = lax.axis_index("pipe")
    r = lax.axis_index("rep")
    zh = r // 8
    x = lax.rem(r // 2, 4)
    c = lax.rem(r, 2)

    def at(zh_, x_, c_):
        return (p, zh_ * 8 + x_ * 2 + c_)

    def x_of(offset):
        return lax.rem(x + offset, 4)

    sibling = at(zh, x, 1 - c)
    partner = at(1 - zh, x, c)
    x_peer = [at(zh, x_of(o), c) for o in OFFSETS[:3]]
    prev = (lax.rem(p + 7, 8), r)
    nxt = (lax.rem(p + 1, 8), r)
    is_last = p == 7

    def cols(start, size):
        return pl.ds(pl.multiple_of(start, GRP), size)

    loads_a, loads_w, loads_u, loads_o = [], [], [], []
    for q in range(4):
        s = pl.ds(q * QTR, QTR)
        loads_a.append(pltpu.make_async_copy(acts.at[0, :, :, s], src.at[0, :, :, s], l_a.at[q]))
        loads_w.append(pltpu.make_async_copy(w_in.at[0, :, s], win_v.at[:, s], l_w.at[q]))
        loads_u.append(pltpu.make_async_copy(ups.at[0, :, s], src.at[1, 0, :, s], l_u.at[q]))
        loads_o.append(pltpu.make_async_copy(w_out.at[0, :, s], wout_v.at[:, s], l_o.at[q]))
    load_mom = pltpu.make_async_copy(mom.at[0], mom_v, l_misc.at[0])
    load_err = pltpu.make_async_copy(err.at[0, 0], err_v, l_misc.at[1])
    load_serr = pltpu.make_async_copy(serr.at[0], serr_v, l_misc.at[2])
    load_fin = pltpu.make_async_copy(fin, src.at[1, 1], l_misc.at[3])
    barrier = pltpu.get_barrier_semaphore()
    for device in [sibling, partner, nxt] + x_peer:
        pl.semaphore_signal(barrier, inc=1, device_id=device, device_id_type=MESH)
    for q in range(2):
        loads_w[q].start()
        loads_a[q].start()
    pl.semaphore_wait(barrier, 6)

    sent = []

    def send(source, target, device):
        copy = pltpu.make_async_remote_copy(
            src_ref=source,
            dst_ref=target,
            send_sem=s_sem.at[len(sent)],
            recv_sem=r_sem.at[len(sent)],
            device_id=device,
            device_id_type=MESH,
        )
        copy.start()
        sent.append(copy)
        return copy

    def finish():
        for copy in sent:
            copy.wait_send()

    def piece(offset, core):
        return cols((x_of(offset) * 2 + core) * PIECE, PIECE)

    wa = [send(w_in.at[0, :, piece(o, c)], wnx_v.at[:, piece(o, c)], prev) for o in (0, 2)]
    for q in range(2, 4):
        loads_w[q].start()
        loads_a[q].start()
    for q in range(4):
        loads_o[q].start()
        loads_u[q].start()

    @pl.when(is_last)
    def _():
        load_fin.start()

    hidden = jnp.zeros((K, 2 * TOK), F32)
    for q in range(4):
        loads_w[q].wait()
        loads_a[q].wait()
        s = pl.ds(q * QTR, QTR)
        hidden = hidden + nt_dot(win_v[:, s], src[0, :, :, s].reshape(2 * TOK, QTR))
    gelu_value, gelu_slope = gelu_parts(hidden)
    factor[1] = gelu_value.astype(BF16)
    slope_v[...] = gelu_slope

    wc = []

    def to_sibling(offset):
        wc.append(send(wnx_v.at[:, piece(offset, c)], wnx_v.at[:, piece(offset, c)], sibling))

    load_mom.start()
    load_err.start()
    load_serr.start()
    wa[0].wait_recv()
    wb = [send(wnx_v.at[:, piece(0, c)], wnx_v.at[:, piece(0, c)], at(zh, x_of(o), c)) for o in (1, 3)]
    to_sibling(0)

    up = jnp.zeros((K, TOK), F32)
    for q in range(4):
        loads_o[q].wait()
        loads_u[q].wait()
        s = pl.ds(q * QTR, QTR)
        up = up + nt_dot(wout_v[:, s], src[1, 0, :, s])
    hg = (up * slope_v[:, :TOK]).astype(BF16)
    factor[0, :, :TOK] = hg
    hg_out[...] = hg
    hg_copy = send(hg_out, hg_next, prev)

    wa[1].wait_recv()
    to_sibling(2)
    wb[0].wait_recv()
    to_sibling(3)
    wb[1].wait_recv()
    to_sibling(1)
    for copy in wc:
        copy.wait_recv()
    hg_copy.wait_recv()

    @pl.when(jnp.logical_not(is_last))
    def _():
        left = hg_next[...].astype(F32).T.astype(BF16)
        up = jnp.zeros((TOK, K), F32)
        for q in range(4):
            s = pl.ds(q * QTR, QTR)
            incoming = nn_dot(left, wnx_v[:, s]).astype(BF16)
            src[1, 1, :, s] = incoming
            up = up + nt_dot(incoming, wout_v[:, s])
        hg1_v[...] = up

    @pl.when(is_last)
    def _():
        load_fin.wait()
        up = jnp.zeros((TOK, K), F32)
        for q in range(4):
            s = pl.ds(q * QTR, QTR)
            up = up + nt_dot(src[1, 1, :, s], wout_v[:, s])
        hg1_v[...] = up

    hg1 = (hg1_v[...].T * slope_v[:, TOK:])
    factor[0, :, TOK:] = hg1.astype(BF16)

    load_mom.wait()
    load_err.wait()

    grads = (grad_a, grad_b)

    def base_of(k, zz):
        return (zz * 8 + x_of(OFFSETS[k]) * 2) * BLK

    def product(k, mat, zz):
        block = cols(base_of(k, zz), TWO)
        grads[zz][...] = nn_dot(factor[mat], src[mat, :, :, block].reshape(2 * TOK, TWO))

    def squeeze(k, mat, zz):
        base = base_of(k, zz)
        for g in range(2 * GROUPS):
            s = cols(base + g * GRP, GRP)
            blended = (
                MOMENTUM_DECAY * mom_v[mat, :, s].astype(F32)
                + (1.0 - MOMENTUM_DECAY) * grads[zz][:, g * GRP : (g + 1) * GRP]
                + err_v[mat, :, s].astype(F32)
            )
            value = compress_group(blended)
            nw_v[mat, :, s] = (blended - value).astype(BF16)
            at_g = g % GROUPS
            v_own[k, mat, g // GROUPS, zz, :, at_g * GRP : (at_g + 1) * GRP] = value.astype(BF16)

    sib = []
    x1c, z1c = [], []
    steps = [(k, mat) for k in range(4) for mat in range(2)]

    def pair(i):
        k, mat = steps[i]
        sib[i].wait_recv()
        for zz in range(2):
            v_sum[k, mat, zz] = (v_own[k, mat, c, zz].astype(F32) + r_sib[k, mat, zz].astype(F32)).astype(BF16)
        if mat == 1:
            z1c.append(send(v_sum.at[k, 1, 1 - zh], z1.at[k], partner))
        elif k < 3:
            x1c.append(send(v_sum.at[k, 0], x1.at[k], x_peer[k]))

    product(0, 0, 0)
    for i, (k, mat) in enumerate(steps):
        product(k, mat, 1)
        squeeze(k, mat, 0)
        if i < 7:
            product(*steps[i + 1], 0)
        squeeze(k, mat, 1)
        sib.append(send(v_own.at[k, mat, 1 - c], r_sib.at[k, mat], sibling))
        if i > 0:
            pair(i - 1)
    pair(7)

    z2c = []
    for k in range(3):
        z1c[k].wait_recv()
        v_sum[k, 1, zh] = (v_sum[k, 1, zh].astype(F32) + z1[k].astype(F32)).astype(BF16)
        z2c.append(send(v_sum.at[k, 1, zh], z2.at[k], x_peer[k]))

    left = hg1.T.astype(BF16)

    for q in range(2):
        s = pl.ds(q * (D // 2), D // 2)
        ig_v[:, s] = nn_dot(left, win_v[:, s]).astype(BF16)
    load_serr.wait()

    for k in range(3):
        x1c[k].wait_recv()
    other = 1 - zh
    v_sum[3, 0, other] = (
        v_sum[3, 0, other].astype(F32)
        + x1[0, other].astype(F32)
        + x1[1, other].astype(F32)
        + x1[2, other].astype(F32)
    ).astype(BF16)
    x2c = send(v_sum.at[3, 0, other], x2, partner)

    my_cols = r * BLK

    def serve(mat, terms):
        for g in range(GROUPS):
            gs = slice(g * GRP, (g + 1) * GRP)
            total = v_sum[3, mat, zh, :, gs].astype(F32)
            for term in terms:
                total = total + term[:, gs].astype(F32)
            combined = total * (1.0 / 16.0) + serr_v[mat, :, gs].astype(F32)
            value = compress_group(combined)
            ns_v[mat, :, gs] = (combined - value).astype(BF16)
            nm_v[mat, :, cols(my_cols + g * GRP, GRP)] = value.astype(BF16)

    z1c[3].wait_recv()
    for k in range(3):
        z2c[k].wait_recv()
    serve(1, [z1.at[3], z2.at[0], z2.at[1], z2.at[2]])
    x2c.wait_recv()
    serve(0, [x1.at[0, zh], x1.at[1, zh], x1.at[2, zh], x2])

    def push(zh_, x_, mat, device, rows=None):
        s = cols((zh_ * 8 + x_ * 2 + c) * BLK, BLK)
        block = nm_v.at[:, :, s] if mat is None else nm_v.at[mat, :, s] if rows is None else nm_v.at[mat, rows, s]
        return send(block, block, device)

    sibs = []

    def share(zh_, x_, mat, rows=None):
        sibs.append(push(zh_, x_, mat, sibling, rows))

    def x_from(offset):
        return x_of(4 - offset)

    x_next = {1: x_peer[1], 3: x_peer[2]}
    part = {1: pl.ds(0, K // 2), 3: pl.ds(K // 2, K // 2)}
    gx1 = {o: push(zh, x, 1, x_next[o]) for o in (1, 3)}
    gz0 = push(zh, x, 0, partner)
    gz1 = push(zh, x, 1, partner)
    gx0 = {o: push(zh, x, 0, x_next[o]) for o in (1, 3)}
    share(zh, x, None)
    gz0.wait_recv()
    hx = {o: push(other, x, 0, x_next[o]) for o in (1, 3)}
    share(other, x, 0)
    hz, far = {}, {}
    for o in (1, 3):
        gx1[o].wait_recv()
        far[1, o] = push(zh, x_from(o), 1, x_next[o], part[o])
        hz[o] = push(zh, x_from(o), 1, partner)
        share(zh, x_from(o), 1)
    gz1.wait_recv()
    share(other, x, 1)
    for o in (1, 3):
        gx0[o].wait_recv()
        far[0, o] = push(zh, x_from(o), 0, x_next[o], part[o])
        share(zh, x_from(o), 0)
    for o in (1, 3):
        far[1, o].wait_recv()
        hz[2, o] = push(zh, x_from(2), 1, partner, part[o])
        share(zh, x_from(2), 1, part[o])
    for o in (1, 3):
        hx[o].wait_recv()
        far[2, o] = push(other, x_from(o), 0, x_next[o], part[o])
        share(other, x_from(o), 0)
    for o in (1, 3):
        hz[o].wait_recv()
        share(other, x_from(o), 1)
        far[0, o].wait_recv()
        share(zh, x_from(2), 0, part[o])
    for o in (1, 3):
        hz[2, o].wait_recv()
        share(other, x_from(2), 1, part[o])
    for o in (1, 3):
        far[2, o].wait_recv()
        share(other, x_from(2), 0, part[o])
    for copy in sibs:
        copy.wait_recv()

    finish()


def store_kernel(a, b, c, d, a_out, b_out, c_out, d_out, sem):
    copies = [
        pltpu.make_async_copy(source, target, sem.at[i])
        for i, (source, target) in enumerate(((a, a_out), (b, b_out), (c, c_out), (d, d_out)))
    ]
    for copy in copies:
        copy.start()
    for copy in copies:
        copy.wait()


def body(*arrays):
    dma = pltpu.SemaphoreType.DMA
    vmem = pltpu.VMEM
    shapes = ((TOK, D), (2, K, D), (2, K, D), (2, K, BLK))
    results = pl.pallas_call(
        kernel,
        name="cascade",
        out_shape=tuple(pltpu.VMEM(shape, BF16) for shape in shapes),
        in_specs=[pl.BlockSpec(memory_space=pl.ANY)] * 8,
        out_specs=(pl.BlockSpec(memory_space=pltpu.VMEM),) * 4,
        scratch_shapes=[
            vmem((2, 2, TOK, D), BF16),
            vmem((K, D), BF16),
            vmem((K, D), BF16),
            vmem((K, D), BF16),
            vmem((2, K, D), BF16),
            vmem((2, K, D), BF16),
            vmem((2, K, BLK), BF16),
            vmem((4, 2, 2, 2, K, BLK), BF16),
            vmem((4, 2, 2, K, BLK), BF16),
            vmem((4, 2, 2, K, BLK), BF16),
            vmem((3, 2, K, BLK), BF16),
            vmem((K, BLK), BF16),
            vmem((4, K, BLK), BF16),
            vmem((3, K, BLK), BF16),
            vmem((K, 2 * TOK), F32),
            vmem((2, K, 2 * TOK), BF16),
            vmem((K, TOK), BF16),
            vmem((K, TOK), BF16),
            vmem((TOK, K), F32),
            vmem((K, TWO), F32),
            vmem((K, TWO), F32),
            dma((4,)), dma((4,)), dma((4,)), dma((4,)), dma((4,)), dma((80,)), dma((80,)),
        ],
        compiler_params=pltpu.CompilerParams(
            collective_id=0, has_side_effects=True, vmem_limit_bytes=44 * 2**20
        ),
        cost_estimate=pl.CostEstimate(flops=2_500_000_000, bytes_accessed=37_000_000, transcendentals=20_000),
    )(*arrays)
    stored = pl.pallas_call(
        store_kernel,
        name="store",
        out_shape=tuple(jax.ShapeDtypeStruct(shape, BF16) for shape in shapes),
        in_specs=[pl.BlockSpec(memory_space=pltpu.VMEM)] * 4,
        out_specs=(pl.BlockSpec(memory_space=pl.ANY),) * 4,
        scratch_shapes=[dma((4,))],
        compiler_params=pltpu.CompilerParams(vmem_limit_bytes=2 * 2**20),
        cost_estimate=pl.CostEstimate(flops=0, bytes_accessed=11_000_000, transcendentals=0),
    )(*results)
    return stored[0][None], stored[1][None], stored[2][None, None], stored[3][None]


def solution(mesh):
    return jax.shard_map(
        body,
        mesh=mesh,
        in_specs=(
            P("pipe", None, "rep", None),
            P("pipe", "rep", None),
            P("rep", None),
            P("pipe", None, None),
            P("pipe", None, None),
            P("pipe", None, None, None),
            P("pipe", "rep", None, None, None),
            P("pipe", None, None, "rep"),
        ),
        out_specs=(
            P("pipe", "rep", None),
            P("pipe", None, None, None),
            P("pipe", "rep", None, None, None),
            P("pipe", None, None, "rep"),
        ),
        check_vma=False,
    )
```

time: 86.7 us -> 69.1 us (0.80); the launches traced: 85.2 us -> 69 us
  local copies, waits for them, and re-layouts: 10.2 us -> 0 us
  Pallas kernels: 74.3 us -> 68.2 us
    unnamed x10 -> x0, local copies, waits for them, and re-layouts: 10.2 us -> none
    pallas_call x1 -> x2, Pallas kernels: 74.3 us -> 68.2 us  [the longest x1 63.9 us: body(): pl.pallas_call(kernel, name='cascade', out_shape=tuple((pltpu.VMEM(shape,...]
where the time goes in v2:
time: 69.1 us; the launch traced here: 69 us
  Pallas kernels  68.2 us (99%)
  between operations  0.8 us (1%)
    pallas_call x1, Pallas kernels, body(): pl.pallas_call(kernel, name='cascade', out_shape=tuple((pltpu.VMEM(shape,...  63.9 us
    pallas_call x1, Pallas kernels, body(): pl.pallas_call(store_kernel, name='store', out_shape=tuple((jax.ShapeDtyp...  4.29 us

profile of v2, /device:TPU:1, one launch (start us, length us, event | category | flops | bytes accessed | tf_op | source)
XLA Modules:
  0.0 69.0 jit_solution(18222950180503105298)
XLA Ops:
  0.6 63.9 %cascade.1 = (bf16[128,14336]{1,0:T(8,128)(2,1)S(1)}, bf16[2,64,14336]{2,1,0:T(8,128)(2,1)S(1)}, bf16[2,64,14336]{2,1,0:T(8,128)(2,1)S(1)}, bf16[2,64,896]{2,1,0:T(8,128)(2,1)S(1)}) custom-call(bf16[1,2,128,14336]{3,2,1,0:T(8,128)(2,1)} %acts.1, bf16[1,128,14336]{2,1,0:T(8,128)(2,1)} %ups.1, bf16[128,14336]{1,0:T(8,128)(2,1)} %fin.1, ...), custom_call_target="tpu_custom_call" | custom-call | flops 2500000000 | bytes 37000000 | tf_op jit(solution)/shard_map/cascade/pallas_call | solution.py:373
  64.5 4.3 %store.1 = (bf16[128,14336]{1,0:T(8,128)(2,1)}, bf16[2,64,14336]{2,1,0:T(8,128)(2,1)}, bf16[2,64,14336]{2,1,0:T(8,128)(2,1)}, bf16[2,64,896]{2,1,0:T(8,128)(2,1)}) custom-call(bf16[128,14336]{1,0:T(8,128)(2,1)S(1)} %get-tuple-element.12.a, bf16[2,64,14336]{2,1,0:T(8,128)(2,1)S(1)} %get-tuple-element.13.b, bf16[2,64,14336]{2,1,0:T(8,128)(2,1)S(1)} %get-tuple-element.14.c, ...), custom_call_target="tpu_custom_call" | custom-call | bytes 11000000 | tf_op jit(solution)/shard_map/store/pallas_call | solution.py:408

commit v3 on v2

--- a/solution.py
+++ b/solution.py
@@ -118,10 +118,11 @@
         for copy in sent:
             copy.wait_send()
 
-    def piece(offset, core):
-        return cols((x_of(offset) * 2 + core) * PIECE, PIECE)
-
-    wa = [send(w_in.at[0, :, piece(o, c)], wnx_v.at[:, piece(o, c)], prev) for o in (0, 2)]
+    def piece(offset, core, part=None):
+        start = (x_of(offset) * 2 + core) * PIECE
+        return cols(start, PIECE) if part is None else cols(start + part * BLK, BLK)
+
+    wa = [send(w_in.at[0, :, s], wnx_v.at[:, s], prev) for s in (piece(0, c, 0), piece(0, c, 1), piece(2, c))]
     for q in range(2, 4):
         loads_w[q].start()
         loads_a[q].start()
@@ -145,15 +146,22 @@
 
     wc = []
 
-    def to_sibling(offset):
-        wc.append(send(wnx_v.at[:, piece(offset, c)], wnx_v.at[:, piece(offset, c)], sibling))
+    def to_sibling(s):
+        wc.append(send(wnx_v.at[:, s], wnx_v.at[:, s], sibling))
+
+    wb = {}
+
+    def spread(i):
+        wa[i].wait_recv()
+        s = piece(0, c, i)
+        for o in (1, 3):
+            wb[i, o] = send(wnx_v.at[:, s], wnx_v.at[:, s], at(zh, x_of(o), c))
+        to_sibling(s)
 
     load_mom.start()
     load_err.start()
     load_serr.start()
-    wa[0].wait_recv()
-    wb = [send(wnx_v.at[:, piece(0, c)], wnx_v.at[:, piece(0, c)], at(zh, x_of(o), c)) for o in (1, 3)]
-    to_sibling(0)
+    spread(0)
 
     up = jnp.zeros((K, TOK), F32)
     for q in range(4):
@@ -166,27 +174,6 @@
     hg_out[...] = hg
     hg_copy = send(hg_out, hg_next, prev)
 
-    wa[1].wait_recv()
-    to_sibling(2)
-    wb[0].wait_recv()
-    to_sibling(3)
-    wb[1].wait_recv()
-    to_sibling(1)
-    for copy in wc:
-        copy.wait_recv()
-    hg_copy.wait_recv()
-
-    @pl.when(jnp.logical_not(is_last))
-    def _():
-        left = hg_next[...].astype(F32).T.astype(BF16)
-        up = jnp.zeros((TOK, K), F32)
-        for q in range(4):
-            s = pl.ds(q * QTR, QTR)
-            incoming = nn_dot(left, wnx_v[:, s]).astype(BF16)
-            src[1, 1, :, s] = incoming
-            up = up + nt_dot(incoming, wout_v[:, s])
-        hg1_v[...] = up
-
     @pl.when(is_last)
     def _():
         load_fin.wait()
@@ -196,7 +183,37 @@
             up = up + nt_dot(src[1, 1, :, s], wout_v[:, s])
         hg1_v[...] = up
 
-    hg1 = (hg1_v[...].T * slope_v[:, TOK:])
+    @pl.when(jnp.logical_not(is_last))
+    def _():
+        hg1_v[...] = jnp.zeros_like(hg1_v)
+
+    spread(1)
+    for i in range(2):
+        wb[i, 1].wait_recv()
+        to_sibling(piece(3, c, i))
+        wb[i, 3].wait_recv()
+        to_sibling(piece(1, c, i))
+    hg_copy.wait_recv()
+    wa[2].wait_recv()
+    to_sibling(piece(2, c))
+
+    def passed_piece(offset, core):
+        @pl.when(jnp.logical_not(is_last))
+        def _():
+            s = piece(offset, core)
+            left = hg_next[...].astype(F32).T.astype(BF16)
+            incoming = nn_dot(left, wnx_v[:, s]).astype(BF16)
+            src[1, 1, :, s] = incoming
+            hg1_v[...] += nt_dot(incoming, wout_v[:, s])
+
+    for offset in (0, 3, 1, 2):
+        passed_piece(offset, c)
+    for offset, arrivals in ((0, (0, 1)), (3, (2, 4)), (1, (3, 5)), (2, (6,))):
+        for i in arrivals:
+            wc[i].wait_recv()
+        passed_piece(offset, 1 - c)
+
+    hg1 = hg1_v[...].T * slope_v[:, TOK:]
     factor[0, :, TOK:] = hg1.astype(BF16)
 
     load_mom.wait()
@@ -229,15 +246,17 @@
     x1c, z1c = [], []
     steps = [(k, mat) for k in range(4) for mat in range(2)]
 
+    other = 1 - zh
+
     def pair(i):
         k, mat = steps[i]
         sib[i].wait_recv()
         for zz in range(2):
             v_sum[k, mat, zz] = (v_own[k, mat, c, zz].astype(F32) + r_sib[k, mat, zz].astype(F32)).astype(BF16)
         if mat == 1:
-            z1c.append(send(v_sum.at[k, 1, 1 - zh], z1.at[k], partner))
+            z1c.append(send(v_sum.at[k, 1, other], z1.at[k], partner))
         elif k < 3:
-            x1c.append(send(v_sum.at[k, 0], x1.at[k], x_peer[k]))
+            x1c.append(send(v_sum.at[k, 0, other], x1.at[k, 0], x_peer[k]))
 
     product(0, 0, 0)
     for i, (k, mat) in enumerate(steps):
@@ -249,32 +268,31 @@
         sib.append(send(v_own.at[k, mat, 1 - c], r_sib.at[k, mat], sibling))
         if i > 0:
             pair(i - 1)
+        if i == 6:
+            x1o = [send(v_sum.at[k, 0, zh], x1.at[k, 1], x_peer[k]) for k in range(3)]
     pair(7)
 
     z2c = []
-    for k in range(3):
+
+    def second(k):
         z1c[k].wait_recv()
         v_sum[k, 1, zh] = (v_sum[k, 1, zh].astype(F32) + z1[k].astype(F32)).astype(BF16)
         z2c.append(send(v_sum.at[k, 1, zh], z2.at[k], x_peer[k]))
 
+    second(0)
     left = hg1.T.astype(BF16)
-
     for q in range(2):
         s = pl.ds(q * (D // 2), D // 2)
         ig_v[:, s] = nn_dot(left, win_v[:, s]).astype(BF16)
-    load_serr.wait()
-
+    second(1)
+    total = v_sum[3, 0, other].astype(F32)
     for k in range(3):
         x1c[k].wait_recv()
-    other = 1 - zh
-    v_sum[3, 0, other] = (
-        v_sum[3, 0, other].astype(F32)
-        + x1[0, other].astype(F32)
-        + x1[1, other].astype(F32)
-        + x1[2, other].astype(F32)
-    ).astype(BF16)
+        total = total + x1[k, 0].astype(F32)
+    v_sum[3, 0, other] = total.astype(BF16)
     x2c = send(v_sum.at[3, 0, other], x2, partner)
-
+    second(2)
+    load_serr.wait()
     my_cols = r * BLK
 
     def serve(mat, terms):
@@ -288,42 +306,44 @@
             ns_v[mat, :, gs] = (combined - value).astype(BF16)
             nm_v[mat, :, cols(my_cols + g * GRP, GRP)] = value.astype(BF16)
 
+    def push(zh_, x_, mat, device, rows=None):
+        s = cols((zh_ * 8 + x_ * 2 + c) * BLK, BLK)
+        block = nm_v.at[:, :, s] if mat is None else nm_v.at[mat, :, s] if rows is None else nm_v.at[mat, rows, s]
+        return send(block, block, device)
+
+    sibs = []
+
+    def share(zh_, x_, mat, rows=None):
+        sibs.append(push(zh_, x_, mat, sibling, rows))
+
+    def x_from(offset):
+        return x_of(4 - offset)
+
+    x_next = {1: x_peer[1], 3: x_peer[2]}
+    part = {1: pl.ds(0, K // 2), 3: pl.ds(K // 2, K // 2)}
     z1c[3].wait_recv()
     for k in range(3):
         z2c[k].wait_recv()
     serve(1, [z1.at[3], z2.at[0], z2.at[1], z2.at[2]])
+    gx1 = {o: push(zh, x, 1, x_next[o]) for o in (1, 3)}
+    gz1 = push(zh, x, 1, partner)
+    share(zh, x, 1)
+    for copy in x1o:
+        copy.wait_recv()
     x2c.wait_recv()
-    serve(0, [x1.at[0, zh], x1.at[1, zh], x1.at[2, zh], x2])
-
-    def push(zh_, x_, mat, device, rows=None):
-        s = cols((zh_ * 8 + x_ * 2 + c) * BLK, BLK)
-        block = nm_v.at[:, :, s] if mat is None else nm_v.at[mat, :, s] if rows is None else nm_v.at[mat, rows, s]
-        return send(block, block, device)
-
-    sibs = []
-
-    def share(zh_, x_, mat, rows=None):
-        sibs.append(push(zh_, x_, mat, sibling, rows))
-
-    def x_from(offset):
-        return x_of(4 - offset)
-
-    x_next = {1: x_peer[1], 3: x_peer[2]}
-    part = {1: pl.ds(0, K // 2), 3: pl.ds(K // 2, K // 2)}
-    gx1 = {o: push(zh, x, 1, x_next[o]) for o in (1, 3)}
+    serve(0, [x1.at[0, 1], x1.at[1, 1], x1.at[2, 1], x2])
     gz0 = push(zh, x, 0, partner)
-    gz1 = push(zh, x, 1, partner)
     gx0 = {o: push(zh, x, 0, x_next[o]) for o in (1, 3)}
-    share(zh, x, None)
-    gz0.wait_recv()
-    hx = {o: push(other, x, 0, x_next[o]) for o in (1, 3)}
-    share(other, x, 0)
+    share(zh, x, 0)
     hz, far = {}, {}
     for o in (1, 3):
         gx1[o].wait_recv()
         far[1, o] = push(zh, x_from(o), 1, x_next[o], part[o])
         hz[o] = push(zh, x_from(o), 1, partner)
         share(zh, x_from(o), 1)
+    gz0.wait_recv()
+    hx = {o: push(other, x, 0, x_next[o]) for o in (1, 3)}
+    share(other, x, 0)
     gz1.wait_recv()
     share(other, x, 1)
     for o in (1, 3):

time: 69.1 us -> 68.6 us (level)
  Pallas kernels: 68.2 us -> 67.1 us
    pallas_call x1, Pallas kernels: 63.9 us -> 62.8 us  [body(): pl.pallas_call(kernel, name='cascade', out_shape=tuple((pltpu.VMEM(shape,...]
where the time goes in v3:
time: 68.6 us; the launch traced here: 67.9 us
  Pallas kernels  67.1 us (98%)
  between operations  0.8 us (1%)
    pallas_call x1, Pallas kernels, body(): pl.pallas_call(kernel, name='cascade', out_shape=tuple((pltpu.VMEM(shape,...  62.8 us
    pallas_call x1, Pallas kernels, body(): pl.pallas_call(store_kernel, name='store', out_shape=tuple((jax.ShapeDtyp...  4.29 us

profile of v3, /device:TPU:1, one launch (start us, length us, event | category | flops | bytes accessed | tf_op | source)
XLA Modules:
  0.0 67.9 jit_solution(7710589589318962497)
XLA Ops:
  0.6 62.8 %cascade.1 = (bf16[128,14336]{1,0:T(8,128)(2,1)S(1)}, bf16[2,64,14336]{2,1,0:T(8,128)(2,1)S(1)}, bf16[2,64,14336]{2,1,0:T(8,128)(2,1)S(1)}, bf16[2,64,896]{2,1,0:T(8,128)(2,1)S(1)}) custom-call(bf16[1,2,128,14336]{3,2,1,0:T(8,128)(2,1)} %acts.1, bf16[1,128,14336]{2,1,0:T(8,128)(2,1)} %ups.1, bf16[128,14336]{1,0:T(8,128)(2,1)} %fin.1, ...), custom_call_target="tpu_custom_call" | custom-call | flops 2500000000 | bytes 37000000 | tf_op jit(solution)/shard_map/cascade/pallas_call | solution.py:393
  63.4 4.3 %store.1 = (bf16[128,14336]{1,0:T(8,128)(2,1)}, bf16[2,64,14336]{2,1,0:T(8,128)(2,1)}, bf16[2,64,14336]{2,1,0:T(8,128)(2,1)}, bf16[2,64,896]{2,1,0:T(8,128)(2,1)}) custom-call(bf16[128,14336]{1,0:T(8,128)(2,1)S(1)} %get-tuple-element.12.a, bf16[2,64,14336]{2,1,0:T(8,128)(2,1)S(1)} %get-tuple-element.13.b, bf16[2,64,14336]{2,1,0:T(8,128)(2,1)S(1)} %get-tuple-element.14.c, ...), custom_call_target="tpu_custom_call" | custom-call | bytes 11000000 | tf_op jit(solution)/shard_map/store/pallas_call | solution.py:428

commit v4 on v3

--- a/solution.py
+++ b/solution.py
@@ -268,7 +268,7 @@
         sib.append(send(v_own.at[k, mat, 1 - c], r_sib.at[k, mat], sibling))
         if i > 0:
             pair(i - 1)
-        if i == 6:
+        if i == 5:
             x1o = [send(v_sum.at[k, 0, zh], x1.at[k, 1], x_peer[k]) for k in range(3)]
     pair(7)
 

time: 68.6 us -> 68.6 us (level)
  no operation moved by 1% of the time
where the time goes in v4:
time: 68.6 us; the launch traced here: 67.9 us
  Pallas kernels  67.1 us (98%)
  between operations  0.8 us (1%)
    pallas_call x1, Pallas kernels, body(): pl.pallas_call(kernel, name='cascade', out_shape=tuple((pltpu.VMEM(shape,...  62.8 us
    pallas_call x1, Pallas kernels, body(): pl.pallas_call(store_kernel, name='store', out_shape=tuple((jax.ShapeDtyp...  4.29 us

profile of v4, /device:TPU:1, one launch (start us, length us, event | category | flops | bytes accessed | tf_op | source)
XLA Modules:
  0.0 67.9 jit_solution(8762718977965845664)
XLA Ops:
  0.6 62.8 %cascade.1 = (bf16[128,14336]{1,0:T(8,128)(2,1)S(1)}, bf16[2,64,14336]{2,1,0:T(8,128)(2,1)S(1)}, bf16[2,64,14336]{2,1,0:T(8,128)(2,1)S(1)}, bf16[2,64,896]{2,1,0:T(8,128)(2,1)S(1)}) custom-call(bf16[1,2,128,14336]{3,2,1,0:T(8,128)(2,1)} %acts.1, bf16[1,128,14336]{2,1,0:T(8,128)(2,1)} %ups.1, bf16[128,14336]{1,0:T(8,128)(2,1)} %fin.1, ...), custom_call_target="tpu_custom_call" | custom-call | flops 2500000000 | bytes 37000000 | tf_op jit(solution)/shard_map/cascade/pallas_call | solution.py:393
  63.4 4.3 %store.1 = (bf16[128,14336]{1,0:T(8,128)(2,1)}, bf16[2,64,14336]{2,1,0:T(8,128)(2,1)}, bf16[2,64,14336]{2,1,0:T(8,128)(2,1)}, bf16[2,64,896]{2,1,0:T(8,128)(2,1)}) custom-call(bf16[128,14336]{1,0:T(8,128)(2,1)S(1)} %get-tuple-element.12.a, bf16[2,64,14336]{2,1,0:T(8,128)(2,1)S(1)} %get-tuple-element.13.b, bf16[2,64,14336]{2,1,0:T(8,128)(2,1)S(1)} %get-tuple-element.14.c, ...), custom_call_target="tpu_custom_call" | custom-call | bytes 11000000 | tf_op jit(solution)/shard_map/store/pallas_call | solution.py:428
